TPU v7x, 768 devices: a whole 4x8x12 slice. The times are simulated.
768 devices in a mesh: row: 48 (over z, y_lo, core), col: 16 (over x, y_hi).
Axes of the slice: x: 4, y: 8 (y_hi: 4, y_lo: 2; y = y_hi * 2 + y_lo), z: 12, core: 2. Of those that a mesh axis runs over, the one named last changes fastest.
Arguments:
- blocks: float32 [144, 16, 4096], P('row', 'col'), may hold values from -0.75 to 0.75
- block_cols: int32 [144, 16], replicated, may hold values from 0 to 8, as said below
- product_cols: int32 [144, 16, 4], replicated, may hold values from 0 to 8, as said below
- group_sizes: int32 [144], replicated, may hold values from 32 to 64, as said below
Outputs:
- purified: float32 [144, 16, 4, 4096], P('row', 'col')
Inputs may be any that keep to these rules, and one draw needn't show every extreme that they name: Block row i holds exactly one stored block in each column segment c, at column c * 9 + block_cols[i, c]. Kept product block (i, c, q) lies at column c * 9 + product_cols[i, c, q]; each is reached by at least one path i to k to j through stored blocks; a column may be kept twice in a segment. `group_sizes`: rows and columns of a block at or past its group size are padding.
All inputs are finite; a program needn't handle non-finite values.
Results may differ from a plain program's by a relative error of at most 0.0003.
Values sent between devices are 32-bit elements; how exact they have to be, the bound alone decides.
A program may use at most 64 MiB of HBM per device.

v0:
```python
import jax
import jax.numpy as jnp
from jax import lax
from jax.sharding import PartitionSpec as P

BS = 64
BSQ = 4096
RB = 3
QS = 4


def block_mask(group_sizes, row_ids, col_ids):
    positions = jnp.arange(BS, dtype=jnp.int32)
    row_live = (positions < jnp.take(group_sizes, row_ids)[..., None]).astype(jnp.float32)
    col_live = (positions < jnp.take(group_sizes, col_ids)[..., None]).astype(jnp.float32)
    return row_live[..., :, None] * col_live[..., None, :]


def per_device(blocks, block_cols, product_cols, group_sizes):
    highest = lax.Precision.HIGHEST
    seg_total = lax.axis_size("col")
    total_rows = RB * lax.axis_size("row")
    seg_len = total_rows // seg_total
    grid_row = lax.axis_index("row")
    segment = lax.axis_index("col")
    my_rows = grid_row * RB + jnp.arange(RB, dtype=jnp.int32)
    my_cols = lax.dynamic_slice_in_dim(block_cols, grid_row * RB, RB, 0)
    my_product = lax.dynamic_slice_in_dim(product_cols, grid_row * RB, RB, 0)
    own_global = segment * seg_len + lax.dynamic_slice_in_dim(my_cols, segment, 1, 1)[:, 0]
    own_tile = blocks[:, 0, :].reshape(RB, BS, BS) * block_mask(group_sizes, my_rows, own_global)
    own_tile = own_tile.reshape(RB, BSQ)
    strip_cols = lax.dynamic_slice_in_dim(block_cols, segment, 1, 1)[:, 0]
    target = lax.dynamic_slice_in_dim(my_product, segment, 1, 1)[:, 0, :]
    column_strip = lax.all_gather(own_tile, "row", axis=0, tiled=True)
    incoming = lax.all_gather(own_tile[None], "col", axis=0, tiled=True)
    pieces = incoming.shape[0]
    segments = jnp.arange(pieces, dtype=jnp.int32)
    local_cols = jnp.transpose(my_cols, (1, 0))
    inner_rows = segments[:, None] * seg_len + local_cols
    right_blocks = jnp.take(column_strip, inner_rows.reshape(-1), axis=0).reshape(
        pieces, RB, BS, BS
    )
    left_blocks = incoming.reshape(pieces, RB, BS, BS)
    products = jnp.einsum("stab,stbd->stad", left_blocks, right_blocks, precision=highest)
    matches = (jnp.take(strip_cols, inner_rows)[:, :, None] == target[None]).astype(jnp.float32)
    added = jnp.einsum("stq,stad->tqad", matches, products, precision=highest)
    square_part = added.reshape(RB, QS, BSQ)
    right_strip = lax.all_gather(own_tile, "row", axis=0, tiled=True)
    incoming = lax.all_gather(square_part[None], "col", axis=0, tiled=True)
    pieces = incoming.shape[0]
    segments = jnp.arange(pieces, dtype=jnp.int32)
    local_cols = jnp.transpose(my_product, (1, 0, 2))
    inner_rows = segments[:, None, None] * seg_len + local_cols
    right_blocks = jnp.take(right_strip, inner_rows.reshape(-1), axis=0).reshape(
        pieces, RB, QS, BS, BS
    )
    left_blocks = incoming.reshape(pieces, RB, QS, BS, BS)
    products = jnp.einsum("stuab,stubd->stuad", left_blocks, right_blocks, precision=highest)
    arrive = jnp.take(strip_cols, inner_rows)
    matches = (arrive[..., None] == target[None, :, None, :]).astype(jnp.float32)
    added = jnp.einsum("stuq,stuad->tqad", matches, products, precision=highest)
    cube_part = added.reshape(RB, QS, BSQ)
    result = 3.0 * square_part - 2.0 * cube_part
    return result[:, None]


def solution(mesh):
    placed = (P("row", "col", None), P(), P(), P())
    return jax.shard_map(
        per_device,
        mesh=mesh,
        in_specs=placed,
        out_specs=P("row", "col", None, None),
        check_vma=False,
    )
```

profile of v0, /device:TPU:2, one launch (start us, length us, event | category | flops | bytes accessed | tf_op | source)
XLA Modules:
  0.0 234.3 jit_solution(12063304107097488903)
XLA Ops:
  6.5 0.8 compare_select_fusion.3
  7.4 1.3 gather_fusion.4
  8.8 1.3 gather_fusion.5
  10.4 1.5 fusion.21
  12.2 0.8 compare_select_fusion.1
  13.2 0.7 constant_dynamic-slice_fusion.2
  13.9 0.8 gather_fusion
  15.0 55.2 %all_gather.10 = f32[16,3,4096]{2,1,0:T(4,128)S(1)} all-gather(f32[1,3,4096]{2,1,0:T(4,128)S(1)} %copy.28), channel_id=1, replica_groups=mesh['row'=48,'col'=16] {'col'}, dimensions={0}, use_global_device_ids=true | all-gather | bytes 835584 | tf_op jit(solution)/shard_map/all_gather | solution.py:35
  70.2 1.9 reshape.299
  72.1 45.2 %all-gather.6.cloned.1.call-done = f32[48,3,4096]{2,1,0:T(4,128)} async-done(((f32[1,3,4096]{2,1,0:T(4,128)}), f32[48,3,4096]{2,1,0:T(4,128)}) %all-gather.6.cloned.1.call-update) | async-done | bytes 2359312 | tf_op jit(solution)/shard_map/all_gather | solution.py:34
  117.4 3.3 %reshape.291 = f32[144,4096]{1,0:T(8,128)S(1)} reshape(f32[48,3,4096]{2,1,0:T(4,128)} %all-gather.6.cloned.1.call-done) | data formatting | bytes 4718592
  120.6 0.8 gather_fusion.1
  121.4 1.8 gather.25
  123.2 3.6 %fusion.8 = f32[16,3,64,64]{3,2,1,0:T(8,128)S(1)} fusion(f32[16,3,64,64]{3,2,1,0:T(8,128)} %reshape.299, f32[16,3,64,64]{3,2,1,0:T(8,128)} %gather.25, pred[16,3]{1,0:T(8,128)(4,1)S(1)} %get-tuple-element.11), kind=kOutput, calls=%fused_computation.14 | convolution fusion | flops 151191552 | bytes 2359344 | tf_op jit(solution)/shard_map/stab,stbd->stad/dot_general | solution.py:44
  126.9 1.5 fusion.6
  128.4 0.9 broadcast_in_dim_reshape.4
  130.0 1.6 gather_fusion.2
  131.8 3.3 %gather_fusion.3 = f32[192,4096]{1,0:T(8,128)} fusion(f32[144,4096]{1,0:T(8,128)S(1)} %reshape.291, s32[1024]{0:T(1024)S(1)} %pad_clamp_fusion), kind=kCustom, calls=%fused_computation.5 | custom fusion | bytes 6292224 | tf_op jit(solution)/shard_map/jit(_take)/gather | solution.py:54
  135.1 6.1 %gather.28 = f32[16,3,4,64,64]{4,3,2,1,0:T(8,128)} reshape(f32[192,4096]{1,0:T(8,128)} %gather_fusion.3) | data formatting | bytes 6291456 | tf_op jit(solution)/shard_map/jit(_take)/gather | solution.py:54
  141.2 63.6 %all-gather.4.cloned.1.call-done = f32[16,3,4,4096]{3,2,1,0:T(4,128)} async-done(((f32[1,3,4,4096]{3,2,1,0:T(4,128)}), f32[16,3,4,4096]{3,2,1,0:T(4,128)}) %all-gather.4.cloned.1.call-update) | async-done | bytes 3145744 | tf_op jit(solution)/shard_map/all_gather | solution.py:49
  204.8 6.4 %reshape.234 = f32[16,3,4,64,64]{4,3,2,1,0:T(8,128)} reshape(f32[16,3,4,4096]{3,2,1,0:T(4,128)} %all-gather.4.cloned.1.call-done) | data formatting | bytes 6291456 | tf_op jit(solution)/shard_map/reshape | solution.py:57
  211.2 9.5 %fusion.2 = f32[16,3,4,64,64]{4,3,2,1,0:T(8,128)S(1)} fusion(f32[16,3,4,64,64]{4,3,2,1,0:T(8,128)} %reshape.234, f32[16,3,4,64,64]{4,3,2,1,0:T(8,128)} %gather.28, pred[16,3,4]{2,1,0:T(4,128)(4,1)S(1)} %get-tuple-element.7), kind=kOutput, calls=%fused_computation.8 | convolution fusion | flops 604766208 | bytes 9437376 | tf_op jit(solution)/shard_map/stuab,stubd->stuad/dot_general | solution.py:58
  220.6 5.9 %fusion.16 = f32[3,4,64,64]{3,1,2,0:T(4,128)S(1)} fusion(f32[16,3,4,64,64]{4,3,2,1,0:T(8,128)S(1)} %fusion.2, f32[3,4,64,64]{3,1,2,0:T(4,128)S(1)} %fusion.6, s32[3,4]{1,0:T(4,128)S(1)} %bitcast.48, s32[16,3,4]{0,2,1:T(4,128)S(1)} %copy.33), kind=kOutput, calls=%fused_computation.18 | convolution fusion | flops 37896960 | bytes 3539760 | tf_op jit(solution)/shard_map/stuq,stuad->tqad/dot_general | solution.py:61
  226.6 0.9 sub.14
  (43 shorter events, 2.1 us)
Async XLA Ops:
  6.5 5.5 %copy-start = (s32[144,16,4]{0,2,1:T(4,128)S(1)}, s32[144,16,4]{0,2,1:T(4,128)}, u32[]{:S(2)}) copy-start(s32[144,16,4]{0,2,1:T(4,128)} %param.8) | copy-start | bytes 110596
  6.5 110.8 %all-gather.6.cloned.1.call-start = ((), (), s32[]{:S(2)}) async-start(), calls=%async_computation.1 | async-start | bytes 3211264 | tf_op jit(solution)/shard_map/all_gather | solution.py:34
  11.9 193.0 %all-gather.4.cloned.1.call-start = ((), (), s32[]{:S(2)}) async-start(), calls=%async_computation | async-start | bytes 3342336 | tf_op jit(solution)/shard_map/all_gather | solution.py:49
  13.9 1.0 copy-start.1
Sparse Core Ops, SparseCore 0:
  12.0 105.3 all-gather.5
  129.5 75.3 all-gather.3
where the time goes:
time: 235 us; the launch traced here: 234 us
  waiting for transfers between devices  109 us (46%)
  blocking collectives  55.2 us (23%)
  local copies, waits for them, and re-layouts  32.5 us (14%)
  matrix products  20.5 us (9%)
  between operations  13.6 us (6%)
  other arithmetic  3.55 us (2%)
    all_gather x1, waiting for transfers between devices, per_device(): incoming = lax.all_gather(square_part[None], 'col', axis=0, tiled=True)  63.6 us
    all_gather x1, blocking collectives, per_device(): incoming = lax.all_gather(own_tile[None], 'col', axis=0, tiled=True)  55.2 us
    all_gather x1, waiting for transfers between devices, per_device(): column_strip = lax.all_gather(own_tile, 'row', axis=0, tiled=True)  45.2 us
    dot_general x1, matrix products, per_device(): jnp.einsum('stuab,stubd->stuad', left_blocks, right_blocks, precision=hig...  9.45 us
    gather x2, local copies, waits for them, and re-layouts, per_device(): jnp.take(right_strip, inner_rows.reshape(-1), axis=0)  9.36 us
    reshape x1, local copies, waits for them, and re-layouts, per_device(): left_blocks = incoming.reshape(pieces, RB, QS, BS, BS)  6.35 us
    dot_general x1, matrix products, per_device(): added = jnp.einsum('stuq,stuad->tqad', matches, products, precision=highest)  5.9 us
  transfers between devices with their start and end apart: 2, of which 2 were waited for; matrix products, arithmetic and copies ran while one was open for 7% of the time, Pallas kernels for 0%

commit v1 on v0

v1 whole, which is shorter than its diff:
```python
import functools

import jax
import jax.numpy as jnp
from jax import lax
from jax.experimental import pallas as pl
from jax.experimental.pallas import tpu as pltpu
from jax.sharding import PartitionSpec as P

RB = 3
NZ = 12
N_COL = 16
SEG = 9
NB = 144
QS = 4
F32 = jnp.float32
BF16 = jnp.bfloat16
MESH = pl.DeviceIdType.MESH

PLUS_PARTS = {0: (0,), 1: (0, 1), 2: (0,), 3: (0, 1)}


def split(v):
    hi = v.astype(BF16)
    return hi, (v - hi.astype(F32)).astype(BF16)


def kernel(
    own_ref, bct_ref, pct_ref, size_ref, out_ref,
    strip, rows, squares, dup_hi, dup_lo, cube, wide,
    send_sem, z_sem, y_sem, sib_sem, row_sem, sq_sem,
):
    r = lax.axis_index("row")
    c = lax.axis_index("col")
    z, l, o = r // 4, (r // 2) % 2, r % 2
    x, h = c // 4, c % 4

    def dev(dz=0, flip_l=False, flip_o=False, dx=0, dh=0):
        zz = lax.rem(z + dz + NZ, NZ)
        ll = 1 - l if flip_l else l
        oo = 1 - o if flip_o else o
        xx = lax.rem(x + dx + 4, 4)
        hh = lax.rem(h + dh + 4, 4)
        return ((zz * 2 + ll) * 2 + oo, xx * 4 + hh)

    neighbours = [
        dev(dz=1), dev(dz=-1), dev(flip_l=True), dev(flip_o=True),
        dev(dx=1), dev(dx=-1), dev(dh=1), dev(dh=-1),
    ]
    barrier = pltpu.get_barrier_semaphore()
    for other in neighbours:
        pl.semaphore_signal(barrier, inc=1, device_id=other, device_id_type=MESH)

    lane = lax.broadcasted_iota(jnp.int32, (32, 128), 1)
    left = lane < 64
    in_row = lax.broadcasted_iota(jnp.int32, (32, 128), 0) + jnp.where(left, 0, 32)
    in_col = lax.rem(lane, 64)

    def turn(v):
        return pltpu.roll(v, 64, 1)

    for b in range(RB):
        t = own_ref[b]
        wide[pl.ds(0, 32, stride=2), :] = t
        wide[pl.ds(1, 32, stride=2), :] = turn(t)
        packed = jnp.where(left, wide[0:32, :], turn(wide[32:64, :]))
        row_size = size_ref[r * RB + b]
        col_size = size_ref[c * SEG + bct_ref[c, r * RB + b]]
        packed = jnp.where((in_row < row_size) & (in_col < col_size), packed, 0.0)
        strip[r * RB + b] = packed
        rows[c, b] = packed

    pl.semaphore_wait(barrier, len(neighbours))

    started = []

    def push(ref, sem, target):
        copy = pltpu.make_async_remote_copy(
            src_ref=ref, dst_ref=ref, send_sem=send_sem.at[len(started)], recv_sem=sem,
            device_id=target, device_id_type=MESH,
        )
        copy.start()
        started.append(copy)

    def arrived(ref, sem):
        pltpu.make_async_remote_copy(
            src_ref=ref, dst_ref=ref, send_sem=send_sem.at[0], recv_sem=sem,
            device_id=neighbours[0], device_id_type=MESH,
        ).wait_recv()

    class Plane:
        def __init__(self, buf, sem, parts):
            self.buf, self.sem, self.parts = buf, sem, parts

        def at(self, dx, dh, part):
            slot = lax.rem(x + dx, 4) * 4 + lax.rem(h + dh, 4)
            lo, n = self.parts[part]
            return self.buf.at[slot, pl.ds(lo, n)]

        def wait(self, dx, dh, part):
            arrived(self.at(dx, dh, part), self.sem.at[(dx * 4 + dh) * 3 + part])

        def send(self, dx, dh, part, ax, step):
            to_dx = (dx - step) % 4 if ax == "x" else dx
            to_dh = (dh - step) % 4 if ax == "h" else dh
            target = dev(dx=step) if ax == "x" else dev(dh=step)
            push(self.at(dx, dh, part), self.sem.at[(to_dx * 4 + to_dh) * 3 + part], target)

        def own(self, part):
            for ax in ("x", "h"):
                for step in (1, -1):
                    self.send(0, 0, part, ax, step)

        def near_h(self, dh, then=None):
            step = 1 if dh == 3 else -1
            for part in range(len(self.parts)):
                self.wait(0, dh, part)
                if (part in PLUS_PARTS[0]) == (step == 1):
                    self.send(0, dh, part, "h", step)
                for side in (1, -1):
                    self.send(0, dh, part, "x", side)
                if then:
                    then(0, dh, part)

        def far_h(self, then=None):
            for part in range(len(self.parts)):
                self.wait(0, 2, part)
                for side in (1, -1):
                    self.send(0, 2, part, "x", side)
                if then:
                    then(0, 2, part)

        def near_x(self, dh, then=None):
            for part in range(len(self.parts)):
                for dx in (3, 1):
                    step = 1 if dx == 3 else -1
                    self.wait(dx, dh, part)
                    if (part in PLUS_PARTS[dh]) == (step == 1):
                        self.send(dx, dh, part, "x", step)
                if then:
                    for dx in (3, 1):
                        then(dx, dh, part)

        def far_x(self, dh, then=None):
            for part in range(len(self.parts)):
                self.wait(2, dh, part)
                if then:
                    then(2, dh, part)

    row_plane = Plane(rows, row_sem, ((0, 1), (1, 1), (2, 1)))
    sq_plane = Plane(squares, sq_sem, ((0, 1), (1, 1), (2, 1)))

    def tile(dz, flip_l, flip_o, lo=0, n=RB):
        zz = lax.rem(z + dz + NZ, NZ)
        ll = 1 - l if flip_l else l
        oo = 1 - o if flip_o else o
        return strip.at[pl.ds(((zz * 2 + ll) * 2 + oo) * RB + lo, n)]

    UNITS = ((False, 0, 1), (False, 1, 2), (True, 0, 1))
    LAST = {1: (1,), -1: (0, 2)}
    half = NZ // 2

    def unit(dz, k):
        flip, lo, n = UNITS[k]
        return tile(dz, flip, False, lo, n)

    def zsem(step, t, k):
        return z_sem.at[((0 if step == 1 else 1) * (half + 1) + t) * 3 + k]

    def ysem(dz):
        return y_sem.at[dz + half]

    def sibsem(dz, flip):
        return sib_sem.at[(dz + half) * 2 + int(flip)]

    def unpack(dz, flip_l, flip_o):
        zz = lax.rem(z + dz + NZ, NZ)
        ll = 1 - l if flip_l else l
        oo = 1 - o if flip_o else o
        first = ((zz * 2 + ll) * 2 + oo) * RB

        def one(b, carry):
            t = strip[first + b]
            s = turn(t)
            for part, v in enumerate((jnp.where(left, t, s), jnp.where(left, s, t))):
                hi, lo = split(v)
                dup_hi[first + b, 2 * part : 2 * part + 2] = hi.reshape(2, 16, 128)
                dup_lo[first + b, 2 * part : 2 * part + 2] = lo.reshape(2, 16, 128)
            return carry

        lax.fori_loop(0, RB, one, 0)

    for k in (0, 1):
        for step in (1, -1):
            push(unit(0, k), zsem(step, 1, k), dev(dz=step))
        if k == 0:
            push(tile(0, False, False, 0, 1), y_sem.at[2 * half + 1], dev(flip_l=True))
    push(tile(0, False, False, 1, 2), ysem(0), dev(flip_l=True))
    for part in range(3):
        row_plane.own(part)
    push(tile(0, False, False), sibsem(0, False), dev(flip_o=True))
    unpack(0, False, False)
    arrived(tile(0, True, False, 0, 1), y_sem.at[2 * half + 1])
    for step in (1, -1):
        push(unit(0, 2), zsem(step, 1, 2), dev(dz=step))

    def other_plane(dz):
        arrived(tile(dz, True, False, 1, 2), ysem(dz))
        push(tile(dz, True, False), sibsem(dz, True), dev(flip_o=True))

    def from_sibling(dz, flip):
        arrived(tile(dz, flip, True), sibsem(dz, flip))
        unpack(dz, flip, True)

    col_events = {
        1: [lambda: row_plane.near_h(3), lambda: row_plane.near_h(1)],
        2: [lambda: row_plane.near_x(0), lambda: row_plane.far_h()],
        3: [lambda: row_plane.near_x(3), lambda: row_plane.near_x(1)],
        4: [lambda: row_plane.near_x(2)],
    }
    for t in range(1, half):
        for k in range(3):
            for step in (1, -1):
                dz = -t * step
                arrived(unit(dz, k), zsem(step, t, k))
                if t + 1 < half or k in LAST[step]:
                    push(unit(dz, k), zsem(step, t + 1, k), dev(dz=step))
                if k == 1:
                    push(tile(dz, False, False, 1, 2), ysem(dz), dev(flip_l=True))
                    push(tile(dz, False, False), sibsem(dz, False), dev(flip_o=True))
        before = [0] if t == 1 else [t - 1, 1 - t]
        for dz in before:
            other_plane(dz)
        for event in col_events.get(t, ()):
            event()
        for dz in (t, -t):
            unpack(dz, False, False)
        for dz in before:
            unpack(dz, True, False)
            from_sibling(dz, False)
        if t >= 2:
            for dz in [0] if t == 2 else [t - 2, 2 - t]:
                from_sibling(dz, True)

    dz = half
    arrived(unit(dz, 1), zsem(1, half, 1))
    push(tile(dz, False, False, 1, 2), ysem(dz), dev(flip_l=True))
    arrived(unit(dz, 0), zsem(-1, half, 0))
    push(tile(dz, False, False), sibsem(dz, False), dev(flip_o=True))
    arrived(unit(dz, 2), zsem(-1, half, 2))
    for d in (half - 1, 1 - half, half):
        other_plane(d)
    for dh in range(4):
        row_plane.far_x(dh)
    unpack(half, False, False)
    for d in (half - 2, 2 - half):
        from_sibling(d, True)
    for d in (half - 1, 1 - half, half):
        unpack(d, True, False)
        from_sibling(d, False)
    for d in (half - 1, 1 - half, half):
        from_sibling(d, True)

    q_of = lax.broadcasted_iota(jnp.int32, (16, 256), 1) // 64

    def targets(row):
        v = jnp.zeros((16, 256), jnp.int32)
        for q in range(QS):
            v = jnp.where(q_of == q, pct_ref[c, q, row], v)
        return v

    def right(inner, target):
        his, los = [], []
        for k in inner:
            m = jnp.where(target == bct_ref[c, k], 1.0, 0.0).astype(BF16)
            for ref, got in ((dup_hi, his), (dup_lo, los)):
                v = ref[k]
                v = jnp.concatenate([v, v], axis=2) * m[None]
                got.append(v.reshape(64, 256))
        return jnp.concatenate(his, axis=0), jnp.concatenate(los, axis=0)

    def product(lhs, inner, target):
        r_hi, r_lo = right(inner, target)
        l_hi, l_lo = split(lhs)
        both = jnp.dot(jnp.concatenate([l_hi, l_lo], axis=0), r_hi, preferred_element_type=F32)
        return both[:64] + both[64:] + jnp.dot(l_hi, r_lo, preferred_element_type=F32)

    for i in range(RB):
        row = r * RB + i
        target = targets(row)

        def square_step(g, acc):
            t = [rows[g * 4 + s, i] for s in range(4)]
            s = [turn(v) for v in t]
            top = [jnp.where(left, t[0], s[1]), jnp.where(left, t[2], s[3])]
            low = [jnp.where(left, s[0], t[1]), jnp.where(left, s[2], t[3])]
            lhs = jnp.concatenate(
                [jnp.concatenate(top, axis=1), jnp.concatenate(low, axis=1)], axis=0
            )
            inner = [(g * 4 + s) * SEG + bct_ref[g * 4 + s, row] for s in range(4)]
            return acc + product(lhs, inner, target)

        squares[c, i] = lax.fori_loop(0, 4, square_step, jnp.zeros((64, 256), F32))
        sq_plane.own(i)

    def cube_step(dx, dh, i, first=False):
        p = lax.rem(x + dx, 4) * 4 + lax.rem(h + dh, 4)
        row = r * RB + i
        inner = [p * SEG + pct_ref[p, u, row] for u in range(QS)]
        v = product(squares[p, i], inner, targets(row))
        cube[i] = v if first else cube[i] + v

    for i in range(RB):
        cube_step(0, 0, i, True)
    sq_plane.near_h(3)
    sq_plane.near_h(1)

    def cubes(*tiles):
        for dx, dh in tiles:
            lax.fori_loop(0, RB, lambda i, k: (cube_step(dx, dh, i), k)[1], 0)

    cubes((0, 3))
    sq_plane.near_x(0)
    cubes((0, 1))
    sq_plane.far_h()
    cubes((3, 0), (1, 0))
    sq_plane.near_x(3)
    cubes((0, 2), (3, 3))
    sq_plane.near_x(1)
    cubes((1, 3), (3, 1))
    sq_plane.far_x(0)
    sq_plane.near_x(2)
    cubes((1, 1), (2, 0))
    sq_plane.far_x(3)
    cubes((3, 2), (1, 2), (2, 3))
    sq_plane.far_x(1)
    cubes((2, 1))
    sq_plane.far_x(2)
    cubes((2, 2))

    for i in range(RB):
        wide2 = 3.0 * squares[c, i] - 2.0 * cube[i]
        for side in range(2):
            wide[:, :] = wide2[:, 128 * side : 128 * side + 128]
            even = wide[pl.ds(0, 32, stride=2), :]
            odd = wide[pl.ds(1, 32, stride=2), :]
            out_ref[i, :, 2 * side, :] = jnp.where(left, even, turn(odd))
            out_ref[i, :, 2 * side + 1, :] = jnp.where(left, turn(even), odd)

    for copy in started:
        copy.wait_send()


def per_device(blocks, block_cols, product_cols, group_sizes):
    vmem = pl.BlockSpec(memory_space=pltpu.VMEM)
    smem = pl.BlockSpec(memory_space=pltpu.SMEM)
    out = pl.pallas_call(
        kernel,
        out_shape=jax.ShapeDtypeStruct((RB, 32, QS, 128), F32),
        in_specs=[vmem, smem, smem, smem],
        out_specs=vmem,
        scratch_shapes=[
            pltpu.VMEM((NB, 32, 128), F32),
            pltpu.VMEM((N_COL, RB, 32, 128), F32),
            pltpu.VMEM((N_COL, RB, 64, 256), F32),
            pltpu.VMEM((NB, 4, 16, 128), BF16),
            pltpu.VMEM((NB, 4, 16, 128), BF16),
            pltpu.VMEM((RB, 64, 256), F32),
            pltpu.VMEM((64, 128), F32),
            pltpu.SemaphoreType.DMA((180,)),
            pltpu.SemaphoreType.DMA((42,)),
            pltpu.SemaphoreType.DMA((14,)),
            pltpu.SemaphoreType.DMA((26,)),
            pltpu.SemaphoreType.DMA((48,)),
            pltpu.SemaphoreType.DMA((48,)),
        ],
        compiler_params=pltpu.CompilerParams(
            collective_id=0, has_side_effects=True, vmem_limit_bytes=32 * 1024 * 1024
        ),
    )(
        blocks.reshape(RB, 32, 128),
        block_cols.T,
        jnp.transpose(product_cols, (1, 2, 0)),
        group_sizes,
    )
    return jnp.transpose(out, (0, 2, 1, 3)).reshape(RB, 1, QS, 4096)


def solution(mesh):
    return jax.shard_map(
        per_device,
        mesh=mesh,
        in_specs=(P("row", "col", None), P(), P(), P()),
        out_specs=P("row", "col", None, None),
        check_vma=False,
    )
```

time: 235 us -> 86.9 us (0.37)
  the two profiles are of different devices: /device:TPU:2 before, /device:TPU:8 now
where the time goes in v1:
time: 86.9 us; the launch traced here: 86.6 us
  Pallas kernels  82.9 us (95%)
  local copies, waits for them, and re-layouts  3.71 us (4%)
    pallas_call x1, Pallas kernels, per_device(): pl.pallas_call(kernel, out_shape=jax.ShapeDtypeStruct((RB, 32, QS, 128),...  82.9 us
    unnamed x9, local copies, waits for them, and re-layouts  3.71 us

profile of v1, /device:TPU:8, one launch (start us, length us, event | category | flops | bytes accessed | tf_op | source)
XLA Modules:
  0.0 86.6 jit_solution(18312861454911518490)
XLA Ops:
  0.0 0.0 copy-start.3
  0.0 0.7 copy-done.3
  0.7 0.0 copy-start
  0.7 0.8 copy-done
  1.5 0.0 copy-start.1
  1.5 0.8 copy-done.1
  2.3 0.0 copy-start.2
  2.3 0.7 copy-done.2
  3.0 82.9 %shard_map.46 = f32[3,32,4,128]{3,2,1,0:T(4,128)S(1)} custom-call(f32[3,32,128]{2,1,0:T(8,128)S(1)} %bitcast.8, s32[16,144]{1,0:T(8,128)S(1)} %bitcast.9, s32[16,4,144]{2,1,0:T(4,128)S(1)} %bitcast.7, s32[144]{0:T(256)S(1)} %copy-done.3), custom_call_target="tpu_custom_call" | custom-call | tf_op jit(solution)/shard_map/pallas_call | solution.py:357
  86.0 0.7 copy.6
Async XLA Ops:
  0.0 0.7 copy-start.3
  0.7 0.8 copy-start
  1.5 0.8 copy-start.1
  2.3 0.7 copy-start.2

commit v2 on v1

--- a/solution.py
+++ b/solution.py
@@ -11,6 +11,7 @@
 NZ = 12
 N_COL = 16
 SEG = 9
+HOP = 3
 NB = 144
 QS = 4
 F32 = jnp.float32
@@ -26,7 +27,8 @@
 
 
 def kernel(
-    own_ref, bct_ref, pct_ref, size_ref, out_ref,
+    own_hbm, bct_hbm, pct_hbm, size_hbm, out_ref,
+    own_ref, bct_ref, pct_ref, size_ref, load_sem,
     strip, rows, squares, dup_hi, dup_lo, cube, wide,
     send_sem, z_sem, y_sem, sib_sem, row_sem, sq_sem,
 ):
@@ -43,9 +45,17 @@
         hh = lax.rem(h + dh + 4, 4)
         return ((zz * 2 + ll) * 2 + oo, xx * 4 + hh)
 
-    neighbours = [
-        dev(dz=1), dev(dz=-1), dev(flip_l=True), dev(flip_o=True),
-        dev(dx=1), dev(dx=-1), dev(dh=1), dev(dh=-1),
+    loads = [
+        pltpu.make_async_copy(src, dst, load_sem.at[k])
+        for k, (src, dst) in enumerate(
+            ((own_hbm, own_ref), (bct_hbm, bct_ref), (size_hbm, size_ref), (pct_hbm, pct_ref))
+        )
+    ]
+    for load in loads:
+        load.start()
+
+    neighbours = [dev(dz=step * k) for k in range(1, HOP + 1) for step in (1, -1)] + [
+        dev(flip_l=True), dev(flip_o=True), dev(dx=1), dev(dx=-1), dev(dh=1), dev(dh=-1),
     ]
     barrier = pltpu.get_barrier_semaphore()
     for other in neighbours:
@@ -58,6 +68,9 @@
 
     def turn(v):
         return pltpu.roll(v, 64, 1)
+
+    for load in loads[:3]:
+        load.wait()
 
     for b in range(RB):
         t = own_ref[b]
@@ -156,16 +169,11 @@
         oo = 1 - o if flip_o else o
         return strip.at[pl.ds(((zz * 2 + ll) * 2 + oo) * RB + lo, n)]
 
-    UNITS = ((False, 0, 1), (False, 1, 2), (True, 0, 1))
-    LAST = {1: (1,), -1: (0, 2)}
     half = NZ // 2
-
-    def unit(dz, k):
-        flip, lo, n = UNITS[k]
-        return tile(dz, flip, False, lo, n)
-
-    def zsem(step, t, k):
-        return z_sem.at[((0 if step == 1 else 1) * (half + 1) + t) * 3 + k]
+    FAR = {1: (0, 1), -1: (1, 2)}
+
+    def zsem(dz, part=0):
+        return z_sem.at[(dz + half) if part == 0 else 2 * half + 1]
 
     def ysem(dz):
         return y_sem.at[dz + half]
@@ -178,88 +186,83 @@
         ll = 1 - l if flip_l else l
         oo = 1 - o if flip_o else o
         first = ((zz * 2 + ll) * 2 + oo) * RB
-
-        def one(b, carry):
+        for b in range(RB):
             t = strip[first + b]
             s = turn(t)
             for part, v in enumerate((jnp.where(left, t, s), jnp.where(left, s, t))):
                 hi, lo = split(v)
                 dup_hi[first + b, 2 * part : 2 * part + 2] = hi.reshape(2, 16, 128)
                 dup_lo[first + b, 2 * part : 2 * part + 2] = lo.reshape(2, 16, 128)
-            return carry
-
-        lax.fori_loop(0, RB, one, 0)
-
-    for k in (0, 1):
-        for step in (1, -1):
-            push(unit(0, k), zsem(step, 1, k), dev(dz=step))
-        if k == 0:
-            push(tile(0, False, False, 0, 1), y_sem.at[2 * half + 1], dev(flip_l=True))
-    push(tile(0, False, False, 1, 2), ysem(0), dev(flip_l=True))
-    for part in range(3):
-        row_plane.own(part)
-    push(tile(0, False, False), sibsem(0, False), dev(flip_o=True))
-    unpack(0, False, False)
-    arrived(tile(0, True, False, 0, 1), y_sem.at[2 * half + 1])
-    for step in (1, -1):
-        push(unit(0, 2), zsem(step, 1, 2), dev(dz=step))
+
+    def across(dz):
+        push(tile(dz, False, False), ysem(dz), dev(flip_l=True))
+        push(tile(dz, False, False), sibsem(dz, False), dev(flip_o=True))
+
+    def near_z(dz):
+        arrived(tile(dz, False, False), zsem(dz))
+        if abs(dz) == HOP:
+            step = 1 if dz < 0 else -1
+            lo, n = FAR[step]
+            push(tile(dz, False, False, lo, n), zsem(half, int(step < 0)), dev(dz=3 * step))
+            for k in (2, 1):
+                push(tile(dz, False, False), zsem(dz - k * step), dev(dz=k * step))
+        across(dz)
 
     def other_plane(dz):
-        arrived(tile(dz, True, False, 1, 2), ysem(dz))
+        arrived(tile(dz, True, False), ysem(dz))
         push(tile(dz, True, False), sibsem(dz, True), dev(flip_o=True))
+        unpack(dz, True, False)
 
     def from_sibling(dz, flip):
         arrived(tile(dz, flip, True), sibsem(dz, flip))
         unpack(dz, flip, True)
 
-    col_events = {
-        1: [lambda: row_plane.near_h(3), lambda: row_plane.near_h(1)],
-        2: [lambda: row_plane.near_x(0), lambda: row_plane.far_h()],
-        3: [lambda: row_plane.near_x(3), lambda: row_plane.near_x(1)],
-        4: [lambda: row_plane.near_x(2)],
-    }
-    for t in range(1, half):
-        for k in range(3):
-            for step in (1, -1):
-                dz = -t * step
-                arrived(unit(dz, k), zsem(step, t, k))
-                if t + 1 < half or k in LAST[step]:
-                    push(unit(dz, k), zsem(step, t + 1, k), dev(dz=step))
-                if k == 1:
-                    push(tile(dz, False, False, 1, 2), ysem(dz), dev(flip_l=True))
-                    push(tile(dz, False, False), sibsem(dz, False), dev(flip_o=True))
-        before = [0] if t == 1 else [t - 1, 1 - t]
-        for dz in before:
-            other_plane(dz)
-        for event in col_events.get(t, ()):
-            event()
-        for dz in (t, -t):
-            unpack(dz, False, False)
-        for dz in before:
-            unpack(dz, True, False)
-            from_sibling(dz, False)
-        if t >= 2:
-            for dz in [0] if t == 2 else [t - 2, 2 - t]:
-                from_sibling(dz, True)
-
-    dz = half
-    arrived(unit(dz, 1), zsem(1, half, 1))
-    push(tile(dz, False, False, 1, 2), ysem(dz), dev(flip_l=True))
-    arrived(unit(dz, 0), zsem(-1, half, 0))
-    push(tile(dz, False, False), sibsem(dz, False), dev(flip_o=True))
-    arrived(unit(dz, 2), zsem(-1, half, 2))
-    for d in (half - 1, 1 - half, half):
-        other_plane(d)
+    for k in range(HOP, 0, -1):
+        for step in (1, -1):
+            push(tile(0, False, False), zsem(-k * step), dev(dz=k * step))
+    across(0)
+    for part in range(3):
+        row_plane.own(part)
+    loads[3].wait()
+    unpack(0, False, False)
+    other_plane(0)
+    from_sibling(0, False)
+    row_plane.near_h(3)
+    row_plane.near_h(1)
+    for dz in (3, -3, 2, -2, 1, -1):
+        near_z(dz)
+    row_plane.near_x(0)
+    for dz in (3, -3, 2, -2, 1, -1):
+        unpack(dz, False, False)
+    row_plane.far_h()
+    from_sibling(0, True)
+    for dz in (3, -3, 2, -2, 1, -1):
+        from_sibling(dz, False)
+    row_plane.near_x(3)
+    row_plane.near_x(1)
+    for dz in (3, -3, 2, -2):
+        other_plane(dz)
+    for dz in (4, -4, 5, -5):
+        near_z(dz)
+    for step in (1, -1):
+        lo, n = FAR[step]
+        arrived(tile(half, False, False, lo, n), zsem(half, int(step < 0)))
+    across(half)
+    row_plane.near_x(2)
+    for dz in (1, -1):
+        other_plane(dz)
+    for dz in (4, -4, 5, -5, 6):
+        unpack(dz, False, False)
+    for dz in (3, -3, 2, -2, 1, -1):
+        from_sibling(dz, True)
     for dh in range(4):
         row_plane.far_x(dh)
-    unpack(half, False, False)
-    for d in (half - 2, 2 - half):
-        from_sibling(d, True)
-    for d in (half - 1, 1 - half, half):
-        unpack(d, True, False)
-        from_sibling(d, False)
-    for d in (half - 1, 1 - half, half):
-        from_sibling(d, True)
+    for dz in (4, -4, 5, -5, 6):
+        from_sibling(dz, False)
+    for dz in (4, -4, 5, -5, 6):
+        other_plane(dz)
+    for dz in (4, -4, 5, -5, 6):
+        from_sibling(dz, True)
 
     q_of = lax.broadcasted_iota(jnp.int32, (16, 256), 1) // 64
 
@@ -285,11 +288,11 @@
         both = jnp.dot(jnp.concatenate([l_hi, l_lo], axis=0), r_hi, preferred_element_type=F32)
         return both[:64] + both[64:] + jnp.dot(l_hi, r_lo, preferred_element_type=F32)
 
-    for i in range(RB):
-        row = r * RB + i
-        target = targets(row)
-
-        def square_step(g, acc):
+    wanted = [targets(r * RB + i) for i in range(RB)]
+
+    def square_step(g, accs):
+        out = []
+        for i in range(RB):
             t = [rows[g * 4 + s, i] for s in range(4)]
             s = [turn(v) for v in t]
             top = [jnp.where(left, t[0], s[1]), jnp.where(left, t[2], s[3])]
@@ -297,27 +300,26 @@
             lhs = jnp.concatenate(
                 [jnp.concatenate(top, axis=1), jnp.concatenate(low, axis=1)], axis=0
             )
-            inner = [(g * 4 + s) * SEG + bct_ref[g * 4 + s, row] for s in range(4)]
-            return acc + product(lhs, inner, target)
-
-        squares[c, i] = lax.fori_loop(0, 4, square_step, jnp.zeros((64, 256), F32))
+            inner = [(g * 4 + s) * SEG + bct_ref[g * 4 + s, r * RB + i] for s in range(4)]
+            out.append(accs[i] + product(lhs, inner, wanted[i]))
+        return tuple(out)
+
+    accs = lax.fori_loop(0, 4, square_step, (jnp.zeros((64, 256), F32),) * RB)
+    for i in range(RB):
+        squares[c, i] = accs[i]
         sq_plane.own(i)
 
-    def cube_step(dx, dh, i, first=False):
-        p = lax.rem(x + dx, 4) * 4 + lax.rem(h + dh, 4)
-        row = r * RB + i
-        inner = [p * SEG + pct_ref[p, u, row] for u in range(QS)]
-        v = product(squares[p, i], inner, targets(row))
-        cube[i] = v if first else cube[i] + v
-
-    for i in range(RB):
-        cube_step(0, 0, i, True)
+    def cubes(*tiles):
+        for dx, dh in tiles:
+            p = lax.rem(x + dx, 4) * 4 + lax.rem(h + dh, 4)
+            for i in range(RB):
+                inner = [p * SEG + pct_ref[p, u, r * RB + i] for u in range(QS)]
+                v = product(squares[p, i], inner, wanted[i])
+                cube[i] = v if (dx, dh) == (0, 0) else cube[i] + v
+
+    cubes((0, 0))
     sq_plane.near_h(3)
     sq_plane.near_h(1)
-
-    def cubes(*tiles):
-        for dx, dh in tiles:
-            lax.fori_loop(0, RB, lambda i, k: (cube_step(dx, dh, i), k)[1], 0)
 
     cubes((0, 3))
     sq_plane.near_x(0)
@@ -353,13 +355,17 @@
 
 def per_device(blocks, block_cols, product_cols, group_sizes):
     vmem = pl.BlockSpec(memory_space=pltpu.VMEM)
-    smem = pl.BlockSpec(memory_space=pltpu.SMEM)
     out = pl.pallas_call(
         kernel,
         out_shape=jax.ShapeDtypeStruct((RB, 32, QS, 128), F32),
-        in_specs=[vmem, smem, smem, smem],
+        in_specs=[pl.BlockSpec(memory_space=pl.ANY)] * 4,
         out_specs=vmem,
         scratch_shapes=[
+            pltpu.VMEM((RB, 32, 128), F32),
+            pltpu.SMEM((N_COL, NB), jnp.int32),
+            pltpu.SMEM((N_COL, QS, NB), jnp.int32),
+            pltpu.SMEM((NB,), jnp.int32),
+            pltpu.SemaphoreType.DMA((4,)),
             pltpu.VMEM((NB, 32, 128), F32),
             pltpu.VMEM((N_COL, RB, 32, 128), F32),
             pltpu.VMEM((N_COL, RB, 64, 256), F32),
@@ -368,14 +374,14 @@
             pltpu.VMEM((RB, 64, 256), F32),
             pltpu.VMEM((64, 128), F32),
             pltpu.SemaphoreType.DMA((180,)),
-            pltpu.SemaphoreType.DMA((42,)),
             pltpu.SemaphoreType.DMA((14,)),
+            pltpu.SemaphoreType.DMA((13,)),
             pltpu.SemaphoreType.DMA((26,)),
             pltpu.SemaphoreType.DMA((48,)),
             pltpu.SemaphoreType.DMA((48,)),
         ],
         compiler_params=pltpu.CompilerParams(
-            collective_id=0, has_side_effects=True, vmem_limit_bytes=32 * 1024 * 1024
+            collective_id=0, has_side_effects=True, vmem_limit_bytes=56 * 1024 * 1024
         ),
     )(
         blocks.reshape(RB, 32, 128),

time: 86.9 us -> 77.8 us (0.90)
  Pallas kernels: 82.9 us -> 76 us
  local copies, waits for them, and re-layouts: 3.71 us -> 1.62 us
    pallas_call x1, Pallas kernels: 82.9 us -> 76 us  [per_device(): pl.pallas_call(kernel, out_shape=jax.ShapeDtypeStruct((RB, 32, QS, 128),...]
    unnamed x9 -> x1, local copies, waits for them, and re-layouts: 3.71 us -> 1.62 us
where the time goes in v2:
time: 77.8 us; the launch traced here: 77.6 us
  Pallas kernels  76 us (98%)
  local copies, waits for them, and re-layouts  1.62 us (2%)
    pallas_call x1, Pallas kernels, per_device(): pl.pallas_call(kernel, out_shape=jax.ShapeDtypeStruct((RB, 32, QS, 128),...  76 us
    unnamed x1, local copies, waits for them, and re-layouts  1.62 us

profile of v2, /device:TPU:8, one launch (start us, length us, event | category | flops | bytes accessed | tf_op | source)
XLA Modules:
  0.0 77.6 jit_solution(14020649851422065791)
XLA Ops:
  0.0 76.0 %shard_map.46 = f32[3,32,4,128]{3,2,1,0:T(4,128)} custom-call(f32[3,32,128]{2,1,0:T(8,128)} %bitcast.8, s32[16,144]{1,0:T(8,128)} %bitcast.9, s32[16,4,144]{2,1,0:T(4,128)} %bitcast.7, s32[144]{0:T(256)} %size_hbm.1), custom_call_target="tpu_custom_call" | custom-call | tf_op jit(solution)/shard_map/pallas_call | solution.py:358
  76.0 1.6 %copy.6 = f32[3,1,4,4096]{3,2,1,0:T(4,128)} copy(f32[3,1,4,4096]{3,2,1,0:T(4,128)} %bitcast.6) | data formatting | bytes 393216

commit v3 on v2

v3 whole, which is shorter than its diff:
```python
import functools

import jax
import jax.numpy as jnp
from jax import lax
from jax.experimental import pallas as pl
from jax.experimental.pallas import tpu as pltpu
from jax.sharding import PartitionSpec as P

RB = 3
NZ = 12
N_COL = 16
SEG = 9
HOP = 3
NB = 144
QS = 4
F32 = jnp.float32
BF16 = jnp.bfloat16
MESH = pl.DeviceIdType.MESH

PLUS_PARTS = {0: (0,), 1: (1, 2), 2: (0,), 3: (1, 2)}


def split(v):
    hi = v.astype(BF16)
    return hi, (v - hi.astype(F32)).astype(BF16)


def kernel(
    own_hbm, bct_hbm, pct_hbm, size_hbm, out_ref,
    own_ref, bct_ref, pct_ref, size_ref, load_sem,
    strip, rows, squares, dup_hi, dup_lo, cube, wide,
    twin_strip, twin_hi, twin_lo, twin_cube, back_cube,
    send_sem, z_sem, y_sem, sib_sem, row_sem, sq_sem,
    twin_sem, twin_z_sem, twin_y_sem, twin_sib_sem, back_sem,
):
    r = lax.axis_index("row")
    c = lax.axis_index("col")
    z, l, o = r // 4, (r // 2) % 2, r % 2
    x, h = c // 4, c % 4

    def dev(dz=0, flip_l=False, flip_o=False, dx=0, dh=0):
        zz = lax.rem(z + dz + NZ, NZ)
        ll = 1 - l if flip_l else l
        oo = 1 - o if flip_o else o
        xx = lax.rem(x + dx + 4, 4)
        hh = lax.rem(h + dh + 4, 4)
        return ((zz * 2 + ll) * 2 + oo, xx * 4 + hh)

    loads = [
        pltpu.make_async_copy(src, dst, load_sem.at[k])
        for k, (src, dst) in enumerate(
            ((own_hbm, own_ref), (bct_hbm, bct_ref), (size_hbm, size_ref), (pct_hbm, pct_ref))
        )
    ]
    for load in loads:
        load.start()

    neighbours = [dev(dz=step * k) for k in range(1, HOP + 1) for step in (1, -1)] + [
        dev(flip_l=True), dev(flip_o=True), dev(dx=1), dev(dx=-1), dev(dh=1), dev(dh=-1),
    ]
    barrier = pltpu.get_barrier_semaphore()
    for other in neighbours:
        pl.semaphore_signal(barrier, inc=1, device_id=other, device_id_type=MESH)

    lane = lax.broadcasted_iota(jnp.int32, (32, 128), 1)
    left = lane < 64
    in_row = lax.broadcasted_iota(jnp.int32, (32, 128), 0) + jnp.where(left, 0, 32)
    in_col = lax.rem(lane, 64)

    def turn(v):
        return pltpu.roll(v, 64, 1)

    for load in loads[:3]:
        load.wait()

    for b in range(RB):
        t = own_ref[b]
        wide[pl.ds(0, 32, stride=2), :] = t
        wide[pl.ds(1, 32, stride=2), :] = turn(t)
        packed = jnp.where(left, wide[0:32, :], turn(wide[32:64, :]))
        row_size = size_ref[r * RB + b]
        col_size = size_ref[c * SEG + bct_ref[c, r * RB + b]]
        packed = jnp.where((in_row < row_size) & (in_col < col_size), packed, 0.0)
        strip[r * RB + b] = packed
        rows[c, b] = packed

    pl.semaphore_wait(barrier, len(neighbours))

    started = []

    def when(cond, body):
        if cond is None:
            body()
        else:
            pl.when(cond)(body)

    def push(ref, sem, target, dst=None, cond=None):
        k = len(started)

        def copy():
            return pltpu.make_async_remote_copy(
                src_ref=ref, dst_ref=ref if dst is None else dst, send_sem=send_sem.at[k],
                recv_sem=sem, device_id=target, device_id_type=MESH,
            )

        started.append((cond, copy))
        when(cond, lambda: copy().start())

    def arrived(ref, sem, cond=None):
        def wait():
            pltpu.make_async_remote_copy(
                src_ref=ref, dst_ref=ref, send_sem=send_sem.at[0], recv_sem=sem,
                device_id=neighbours[0], device_id_type=MESH,
            ).wait_recv()

        when(cond, wait)

    class Plane:
        def __init__(self, buf, sem, parts):
            self.buf, self.sem, self.parts = buf, sem, parts

        def at(self, dx, dh, part):
            slot = lax.rem(x + dx, 4) * 4 + lax.rem(h + dh, 4)
            lo, n = self.parts[part]
            return self.buf.at[slot, pl.ds(lo, n)]

        def wait(self, dx, dh, part):
            arrived(self.at(dx, dh, part), self.sem.at[(dx * 4 + dh) * len(self.parts) + part])

        def send(self, dx, dh, part, ax, step):
            to_dx = (dx - step) % 4 if ax == "x" else dx
            to_dh = (dh - step) % 4 if ax == "h" else dh
            target = dev(dx=step) if ax == "x" else dev(dh=step)
            sem = self.sem.at[(to_dx * 4 + to_dh) * len(self.parts) + part]
            push(self.at(dx, dh, part), sem, target)

        def both(self, dx, dh, part, ax):
            for step in (1, -1):
                self.send(dx, dh, part, ax, step)

        def own(self, part):
            self.both(0, 0, part, "h")
            self.both(0, 0, part, "x")

        def near_h(self, dh, part):
            step = 1 if dh == 3 else -1
            self.wait(0, dh, part)
            if (part in PLUS_PARTS[0]) == (step == 1):
                self.send(0, dh, part, "h", step)
            self.both(0, dh, part, "x")

        def far_h(self, part):
            self.wait(0, 2, part)
            self.both(0, 2, part, "x")

        def near_x(self, dh, part):
            for dx in (3, 1):
                step = 1 if dx == 3 else -1
                self.wait(dx, dh, part)
                if (part in PLUS_PARTS[dh]) == (step == 1):
                    self.send(dx, dh, part, "x", step)

    THREE = (0, 1, 2)
    row_plane = Plane(rows, row_sem, ((0, 1), (1, 1), (2, 1)))

    half = NZ // 2
    FAR = {1: (0, 1), -1: (1, 2)}

    class Strip:
        def __init__(self, buf, hi, lo, z_sem, y_sem, sib_sem, held):
            self.buf, self.hi, self.lo, self.held = buf, hi, lo, held
            self.z_sem, self.y_sem, self.sib_sem = z_sem, y_sem, sib_sem

        def index(self, dz, flip_l, flip_o):
            zz = lax.rem(z + dz + NZ, NZ)
            ll = 1 - l if flip_l else l
            oo = 1 - o if flip_o else o
            return (zz * 2 + ll) * 2 + oo

        def tile(self, dz, flip_l, flip_o, lo=0, n=RB):
            return self.buf.at[pl.ds(self.index(dz, flip_l, flip_o) * RB + lo, n)]

        def cond(self, dz, flip_l, flip_o):
            return self.held(self.index(dz, flip_l, flip_o)) if self.held else None

        def z_at(self, dz, part=0):
            return self.z_sem.at[(dz + half) if part == 0 else 2 * half + 1]

        def sib_at(self, dz, flip):
            return self.sib_sem.at[(dz + half) * 2 + int(flip)]

        def unpack(self, dz, flip_l, flip_o):
            def body():
                first = self.index(dz, flip_l, flip_o) * RB
                for b in range(RB):
                    t = self.buf[first + b]
                    s = turn(t)
                    for part, v in enumerate((jnp.where(left, t, s), jnp.where(left, s, t))):
                        hi, lo = split(v)
                        self.hi[first + b, 2 * part : 2 * part + 2] = hi.reshape(2, 16, 128)
                        self.lo[first + b, 2 * part : 2 * part + 2] = lo.reshape(2, 16, 128)

            when(self.cond(dz, flip_l, flip_o), body)

        def start_z(self):
            cond = self.cond(0, False, False)
            for k in range(HOP, 0, -1):
                for step in (1, -1):
                    push(self.tile(0, False, False), self.z_at(-k * step), dev(dz=k * step), cond=cond)

        def across(self, dz):
            cond, t = self.cond(dz, False, False), self.tile(dz, False, False)
            push(t, self.y_sem.at[dz + half], dev(flip_l=True), cond=cond)
            push(t, self.sib_at(dz, False), dev(flip_o=True), cond=cond)

        def near_z(self, dz):
            cond, t = self.cond(dz, False, False), self.tile(dz, False, False)
            arrived(t, self.z_at(dz), cond)
            if abs(dz) == HOP:
                step = 1 if dz < 0 else -1
                part = self.tile(dz, False, False, *FAR[step])
                push(part, self.z_at(half, int(step < 0)), dev(dz=3 * step), cond=cond)
                for k in (2, 1):
                    push(t, self.z_at(dz - k * step), dev(dz=k * step), cond=cond)
            self.across(dz)

        def opposite(self):
            for step in (1, -1):
                part = self.tile(half, False, False, *FAR[step])
                arrived(part, self.z_at(half, int(step < 0)), self.cond(half, False, False))
            self.across(half)

        def other_plane(self, dz):
            cond, t = self.cond(dz, True, False), self.tile(dz, True, False)
            arrived(t, self.y_sem.at[dz + half], cond)
            push(t, self.sib_at(dz, True), dev(flip_o=True), cond=cond)
            self.unpack(dz, True, False)

        def from_sibling(self, dz, flip):
            arrived(self.tile(dz, flip, True), self.sib_at(dz, flip), self.cond(dz, flip, True))
            self.unpack(dz, flip, True)

    NEAR = (3, -3, 2, -2, 1, -1)
    FARTHER = (4, -4, 5, -5)
    main = Strip(strip, dup_hi, dup_lo, z_sem, y_sem, sib_sem, None)

    g = h // 2
    twin = (r, x * 4 + 3 - h)
    twin_c = x * 4 + 3 - h

    def held(index):
        return lax.rem(index // 6, 2) == g

    mine = held(r)
    other = Strip(twin_strip, twin_hi, twin_lo, twin_z_sem, twin_y_sem, twin_sib_sem, held)

    main.start_z()
    main.across(0)
    for part in THREE:
        row_plane.own(part)
    own_tile = main.tile(0, False, False)
    push(own_tile, twin_sem.at[0], twin, dst=other.tile(0, False, False), cond=jnp.logical_not(mine))
    loads[3].wait()
    main.unpack(0, False, False)
    main.other_plane(0)
    main.from_sibling(0, False)
    for dh in (3, 1):
        for part in THREE:
            row_plane.near_h(dh, part)
    for dz in NEAR:
        main.near_z(dz)
    arrived(other.tile(0, False, False), twin_sem.at[0], mine)
    other.start_z()
    for part in THREE:
        row_plane.near_x(0, part)
    for dz in NEAR:
        main.unpack(dz, False, False)
    for part in THREE:
        row_plane.far_h(part)
    main.from_sibling(0, True)
    for dz in NEAR:
        main.from_sibling(dz, False)
    for dh in (3, 1):
        for part in THREE:
            row_plane.near_x(dh, part)
    for dz in (3, -3, 2, -2):
        main.other_plane(dz)
    for dz in FARTHER:
        main.near_z(dz)
    main.opposite()
    for part in THREE:
        row_plane.near_x(2, part)
    for dz in NEAR:
        other.near_z(dz)
    other.across(0)
    for dz in (1, -1):
        main.other_plane(dz)
    for dz in FARTHER + (6,):
        main.unpack(dz, False, False)
    for dz in NEAR:
        main.from_sibling(dz, True)
    for dh in range(4):
        for part in THREE:
            row_plane.wait(2, dh, part)
    for dz in FARTHER + (6,):
        main.from_sibling(dz, False)
    for dz in FARTHER + (6,):
        main.other_plane(dz)
    for dz in FARTHER:
        other.near_z(dz)
    other.opposite()
    for dz in FARTHER + (6,):
        main.from_sibling(dz, True)

    q_of = lax.broadcasted_iota(jnp.int32, (16, 256), 1) // 64

    def targets(col, row):
        v = jnp.zeros((16, 256), jnp.int32)
        for q in range(QS):
            v = jnp.where(q_of == q, pct_ref[col, q, row], v)
        return v

    def right(inner, target, col, hi_ref, lo_ref):
        his, los = [], []
        for k in inner:
            m = jnp.where(target == bct_ref[col, k], 1.0, 0.0).astype(BF16)
            for ref, got in ((hi_ref, his), (lo_ref, los)):
                v = ref[k]
                v = jnp.concatenate([v, v], axis=2) * m[None]
                got.append(v.reshape(64, 256))
        return jnp.concatenate(his, axis=0), jnp.concatenate(los, axis=0)

    def product(lhs, inner, target, col=c, hi_ref=dup_hi, lo_ref=dup_lo):
        r_hi, r_lo = right(inner, target, col, hi_ref, lo_ref)
        l_hi, l_lo = split(lhs)
        both = jnp.dot(jnp.concatenate([l_hi, l_lo], axis=0), r_hi, preferred_element_type=F32)
        return both[:64] + both[64:] + jnp.dot(l_hi, r_lo, preferred_element_type=F32)

    wanted = [targets(c, r * RB + i) for i in range(RB)]
    twin_wanted = [targets(twin_c, r * RB + i) for i in range(RB)]

    def square_step(g, accs):
        out = []
        for i in range(RB):
            t = [rows[g * 4 + s, i] for s in range(4)]
            s = [turn(v) for v in t]
            top = [jnp.where(left, t[0], s[1]), jnp.where(left, t[2], s[3])]
            low = [jnp.where(left, s[0], t[1]), jnp.where(left, s[2], t[3])]
            lhs = jnp.concatenate(
                [jnp.concatenate(top, axis=1), jnp.concatenate(low, axis=1)], axis=0
            )
            inner = [(g * 4 + s) * SEG + bct_ref[g * 4 + s, r * RB + i] for s in range(4)]
            out.append(accs[i] + product(lhs, inner, wanted[i]))
        return tuple(out)

    accs = lax.fori_loop(0, 4, square_step, (jnp.zeros((64, 256), F32),) * RB)
    mate_h = h + 1 - 2 * lax.rem(h, 2)
    mate = (r, x * 4 + mate_h)

    def slot(dx, e):
        return lax.rem(x + dx, 4) * 4 + (mate_h if e else h)

    def sq_at(dx, e, i):
        return squares.at[slot(dx, e), pl.ds(64 * i, 64)]

    def sq_sem_at(dx, e, i):
        return sq_sem.at[(dx * 2 + e) * 3 + i]

    def sq_wait(dx, e, i):
        arrived(sq_at(dx, e, i), sq_sem_at(dx, e, i))

    def sq_along_x(e, i):
        for step in (1, -1):
            push(sq_at(0, e, i), sq_sem_at(-step % 4, e, i), dev(dx=step))

    def sq_near_x(e, i):
        for dx in (3, 1):
            step = 1 if dx == 3 else -1
            sq_wait(dx, e, i)
            if (i in PLUS_PARTS[e]) == (step == 1):
                push(sq_at(dx, e, i), sq_sem_at(2, e, i), dev(dx=step))

    def cubes(i, *tiles):
        row = r * RB + i
        for dx, e in tiles:
            p = slot(dx, e)
            lhs = squares[p, pl.ds(64 * i, 64)]
            inner = [p * SEG + pct_ref[p, u, row] for u in range(QS)]
            v = product(lhs, inner, wanted[i])
            w = product(lhs, inner, twin_wanted[i], twin_c, twin_hi, twin_lo)
            first = (dx, e) == (0, 0)
            cube[i] = v if first else cube[i] + v
            twin_cube[i] = w if first else twin_cube[i] + w

    for i in range(RB):
        squares[c, pl.ds(64 * i, 64)] = accs[i]
        push(sq_at(0, 0, i), sq_sem_at(0, 1, i), mate)
        sq_along_x(0, i)
    ALL = (0,) + NEAR + FARTHER + (6,)
    for dz in ALL:
        other.unpack(dz, False, False)
    for dz in ALL[:7]:
        other.from_sibling(dz, False)
    for i in range(RB):
        sq_near_x(0, i)
        sq_wait(0, 1, i)
        sq_along_x(1, i)
    for dz in ALL:
        other.other_plane(dz)
    for dz in ALL[7:]:
        other.from_sibling(dz, False)
    for i in range(RB):
        sq_near_x(1, i)
    for dz in ALL:
        other.from_sibling(dz, True)
    for i in range(RB):
        cubes(i, (0, 0), (3, 0), (1, 0), (0, 1))
    for i in range(RB):
        sq_wait(2, 0, i)
        sq_wait(2, 1, i)
        cubes(i, (2, 0), (3, 1), (1, 1), (2, 1))
        push(twin_cube.at[i], back_sem.at[i], twin, dst=back_cube.at[i])
    for i in range(RB):
        arrived(back_cube.at[i], back_sem.at[i])

    for i in range(RB):
        wide2 = 3.0 * squares[c, pl.ds(64 * i, 64)] - 2.0 * (cube[i] + back_cube[i])
        for side in range(2):
            wide[:, :] = wide2[:, 128 * side : 128 * side + 128]
            even = wide[pl.ds(0, 32, stride=2), :]
            odd = wide[pl.ds(1, 32, stride=2), :]
            out_ref[i, :, 2 * side, :] = jnp.where(left, even, turn(odd))
            out_ref[i, :, 2 * side + 1, :] = jnp.where(left, turn(even), odd)

    for cond, copy in started:
        when(cond, lambda copy=copy: copy().wait_send())


def per_device(blocks, block_cols, product_cols, group_sizes):
    vmem = pl.BlockSpec(memory_space=pltpu.VMEM)
    out = pl.pallas_call(
        kernel,
        out_shape=jax.ShapeDtypeStruct((RB, 32, QS, 128), F32),
        in_specs=[pl.BlockSpec(memory_space=pl.ANY)] * 4,
        out_specs=vmem,
        scratch_shapes=[
            pltpu.VMEM((RB, 32, 128), F32),
            pltpu.SMEM((N_COL, NB), jnp.int32),
            pltpu.SMEM((N_COL, QS, NB), jnp.int32),
            pltpu.SMEM((NB,), jnp.int32),
            pltpu.SemaphoreType.DMA((4,)),
            pltpu.VMEM((NB, 32, 128), F32),
            pltpu.VMEM((N_COL, RB, 32, 128), F32),
            pltpu.VMEM((N_COL, RB * 64, 256), F32),
            pltpu.VMEM((NB, 4, 16, 128), BF16),
            pltpu.VMEM((NB, 4, 16, 128), BF16),
            pltpu.VMEM((RB, 64, 256), F32),
            pltpu.VMEM((64, 128), F32),
            pltpu.VMEM((NB, 32, 128), F32),
            pltpu.VMEM((NB, 4, 16, 128), BF16),
            pltpu.VMEM((NB, 4, 16, 128), BF16),
            pltpu.VMEM((RB, 64, 256), F32),
            pltpu.VMEM((RB, 64, 256), F32),
            pltpu.SemaphoreType.DMA((180,)),
            pltpu.SemaphoreType.DMA((14,)),
            pltpu.SemaphoreType.DMA((13,)),
            pltpu.SemaphoreType.DMA((26,)),
            pltpu.SemaphoreType.DMA((48,)),
            pltpu.SemaphoreType.DMA((24,)),
            pltpu.SemaphoreType.DMA((1,)),
            pltpu.SemaphoreType.DMA((14,)),
            pltpu.SemaphoreType.DMA((13,)),
            pltpu.SemaphoreType.DMA((26,)),
            pltpu.SemaphoreType.DMA((3,)),
        ],
        compiler_params=pltpu.CompilerParams(
            collective_id=0, has_side_effects=True, vmem_limit_bytes=56 * 1024 * 1024
        ),
    )(
        blocks.reshape(RB, 32, 128),
        block_cols.T,
        jnp.transpose(product_cols, (1, 2, 0)),
        group_sizes,
    )
    return jnp.transpose(out, (0, 2, 1, 3)).reshape(RB, 1, QS, 4096)


def solution(mesh):
    return jax.shard_map(
        per_device,
        mesh=mesh,
        in_specs=(P("row", "col", None), P(), P(), P()),
        out_specs=P("row", "col", None, None),
        check_vma=False,
    )
```

time: 77.8 us -> 73.9 us (0.950)
  the two profiles are of different devices: /device:TPU:8 before, /device:TPU:17 now
where the time goes in v3:
time: 73.9 us; the launch traced here: 73.7 us
  Pallas kernels  72.1 us (98%)
  local copies, waits for them, and re-layouts  1.62 us (2%)
    pallas_call x1, Pallas kernels, per_device(): pl.pallas_call(kernel, out_shape=jax.ShapeDtypeStruct((RB, 32, QS, 128),...  72.1 us
    unnamed x1, local copies, waits for them, and re-layouts  1.62 us

profile of v3, /device:TPU:17, one launch (start us, length us, event | category | flops | bytes accessed | tf_op | source)
XLA Modules:
  0.0 73.7 jit_solution(13110809832826417726)
XLA Ops:
  0.0 72.1 %shard_map.46 = f32[3,32,4,128]{3,2,1,0:T(4,128)} custom-call(f32[3,32,128]{2,1,0:T(8,128)} %bitcast.8, s32[16,144]{1,0:T(8,128)} %bitcast.9, s32[16,4,144]{2,1,0:T(4,128)} %bitcast.7, s32[144]{0:T(256)} %size_hbm.1), custom_call_target="tpu_custom_call" | custom-call | tf_op jit(solution)/shard_map/pallas_call | solution.py:442
  72.1 1.6 %copy.6 = f32[3,1,4,4096]{3,2,1,0:T(4,128)} copy(f32[3,1,4,4096]{3,2,1,0:T(4,128)} %bitcast.6) | data formatting | bytes 393216

commit v4 on v3

--- a/solution.py
+++ b/solution.py
@@ -12,6 +12,7 @@
 N_COL = 16
 SEG = 9
 HOP = 3
+ONWARD = {3: (3, 2, 1)}
 NB = 144
 QS = 4
 F32 = jnp.float32
@@ -32,7 +33,7 @@
     strip, rows, squares, dup_hi, dup_lo, cube, wide,
     twin_strip, twin_hi, twin_lo, twin_cube, back_cube,
     send_sem, z_sem, y_sem, sib_sem, row_sem, sq_sem,
-    twin_sem, twin_z_sem, twin_y_sem, twin_sib_sem, back_sem,
+    twin_sem, twin_z_sem, twin_sib_sem, back_sem,
 ):
     r = lax.axis_index("row")
     c = lax.axis_index("col")
@@ -58,6 +59,7 @@
 
     neighbours = [dev(dz=step * k) for k in range(1, HOP + 1) for step in (1, -1)] + [
         dev(flip_l=True), dev(flip_o=True), dev(dx=1), dev(dx=-1), dev(dh=1), dev(dh=-1),
+        (dev(flip_l=True)[0], x * 4 + 3 - h),
     ]
     barrier = pltpu.get_barrier_semaphore()
     for other in neighbours:
@@ -184,8 +186,9 @@
         def cond(self, dz, flip_l, flip_o):
             return self.held(self.index(dz, flip_l, flip_o)) if self.held else None
 
-        def z_at(self, dz, part=0):
-            return self.z_sem.at[(dz + half) if part == 0 else 2 * half + 1]
+        def z_at(self, dz, part=0, flip=False):
+            k = (dz + half) if part == 0 else 2 * half + 1
+            return self.z_sem.at[k + (2 * half + 2 if flip else 0)]
 
         def sib_at(self, dz, flip):
             return self.sib_sem.at[(dz + half) * 2 + int(flip)]
@@ -203,33 +206,46 @@
 
             when(self.cond(dz, flip_l, flip_o), body)
 
-        def start_z(self):
-            cond = self.cond(0, False, False)
-            for k in range(HOP, 0, -1):
+        def start_z(self, flip=False):
+            cond, t = self.cond(0, flip, False), self.tile(0, flip, False)
+            for k in (1, 3, 2):
                 for step in (1, -1):
-                    push(self.tile(0, False, False), self.z_at(-k * step), dev(dz=k * step), cond=cond)
+                    push(t, self.z_at(-k * step, 0, flip), dev(dz=k * step), cond=cond)
+
+        def to_sibling(self, dz, flip):
+            cond, t = self.cond(dz, flip, False), self.tile(dz, flip, False)
+            push(t, self.sib_at(dz, flip), dev(flip_o=True), cond=cond)
 
         def across(self, dz):
-            cond, t = self.cond(dz, False, False), self.tile(dz, False, False)
-            push(t, self.y_sem.at[dz + half], dev(flip_l=True), cond=cond)
-            push(t, self.sib_at(dz, False), dev(flip_o=True), cond=cond)
+            t = self.tile(dz, False, False)
+            push(t, self.y_sem.at[dz + half], dev(flip_l=True))
+            self.to_sibling(dz, False)
+
+        def from_z(self, dz, flip=False):
+            cond, t = self.cond(dz, flip, False), self.tile(dz, flip, False)
+            arrived(t, self.z_at(dz, 0, flip), cond)
+            step = 1 if dz < 0 else -1
+            for k in ONWARD.get(abs(dz), ()):
+                if abs(dz) + k == half:
+                    part = self.tile(dz, flip, False, *FAR[step])
+                    push(part, self.z_at(half, int(step < 0), flip), dev(dz=k * step), cond=cond)
+                else:
+                    push(t, self.z_at(dz - k * step, 0, flip), dev(dz=k * step), cond=cond)
 
         def near_z(self, dz):
-            cond, t = self.cond(dz, False, False), self.tile(dz, False, False)
-            arrived(t, self.z_at(dz), cond)
-            if abs(dz) == HOP:
-                step = 1 if dz < 0 else -1
-                part = self.tile(dz, False, False, *FAR[step])
-                push(part, self.z_at(half, int(step < 0)), dev(dz=3 * step), cond=cond)
-                for k in (2, 1):
-                    push(t, self.z_at(dz - k * step), dev(dz=k * step), cond=cond)
+            self.from_z(dz)
             self.across(dz)
 
-        def opposite(self):
+        def both_from_z(self, dz):
+            for flip in (False, True):
+                self.from_z(dz, flip)
+            for flip in (False, True):
+                self.to_sibling(dz, flip)
+
+        def opposite_from_z(self, flip=False):
             for step in (1, -1):
-                part = self.tile(half, False, False, *FAR[step])
-                arrived(part, self.z_at(half, int(step < 0)), self.cond(half, False, False))
-            self.across(half)
+                part = self.tile(half, flip, False, *FAR[step])
+                arrived(part, self.z_at(half, int(step < 0), flip), self.cond(half, flip, False))
 
         def other_plane(self, dz):
             cond, t = self.cond(dz, True, False), self.tile(dz, True, False)
@@ -241,7 +257,7 @@
             arrived(self.tile(dz, flip, True), self.sib_at(dz, flip), self.cond(dz, flip, True))
             self.unpack(dz, flip, True)
 
-    NEAR = (3, -3, 2, -2, 1, -1)
+    NEAR = (1, -1, 3, -3, 2, -2)
     FARTHER = (4, -4, 5, -5)
     main = Strip(strip, dup_hi, dup_lo, z_sem, y_sem, sib_sem, None)
 
@@ -253,14 +269,16 @@
         return lax.rem(index // 6, 2) == g
 
     mine = held(r)
-    other = Strip(twin_strip, twin_hi, twin_lo, twin_z_sem, twin_y_sem, twin_sib_sem, held)
+    other = Strip(twin_strip, twin_hi, twin_lo, twin_z_sem, None, twin_sib_sem, held)
 
     main.start_z()
     main.across(0)
     for part in THREE:
         row_plane.own(part)
     own_tile = main.tile(0, False, False)
-    push(own_tile, twin_sem.at[0], twin, dst=other.tile(0, False, False), cond=jnp.logical_not(mine))
+    for k, target in enumerate((twin, neighbours[-1])):
+        there = other.tile(0, False, False)
+        push(own_tile, twin_sem.at[k], target, dst=there, cond=jnp.logical_not(mine))
     loads[3].wait()
     main.unpack(0, False, False)
     main.other_plane(0)
@@ -270,8 +288,6 @@
             row_plane.near_h(dh, part)
     for dz in NEAR:
         main.near_z(dz)
-    arrived(other.tile(0, False, False), twin_sem.at[0], mine)
-    other.start_z()
     for part in THREE:
         row_plane.near_x(0, part)
     for dz in NEAR:
@@ -284,17 +300,21 @@
     for dh in (3, 1):
         for part in THREE:
             row_plane.near_x(dh, part)
-    for dz in (3, -3, 2, -2):
+    for dz in (1, -1, 3, -3):
         main.other_plane(dz)
     for dz in FARTHER:
         main.near_z(dz)
-    main.opposite()
+    main.opposite_from_z()
+    main.across(half)
+    for k in (0, 1):
+        flip = k == 1
+        arrived(other.tile(0, flip, False), twin_sem.at[k], other.cond(0, flip, False))
+        other.start_z(flip)
     for part in THREE:
         row_plane.near_x(2, part)
-    for dz in NEAR:
-        other.near_z(dz)
-    other.across(0)
-    for dz in (1, -1):
+    for flip in (False, True):
+        other.to_sibling(0, flip)
+    for dz in (2, -2):
         main.other_plane(dz)
     for dz in FARTHER + (6,):
         main.unpack(dz, False, False)
@@ -307,9 +327,6 @@
         main.from_sibling(dz, False)
     for dz in FARTHER + (6,):
         main.other_plane(dz)
-    for dz in FARTHER:
-        other.near_z(dz)
-    other.opposite()
     for dz in FARTHER + (6,):
         main.from_sibling(dz, True)
 
@@ -340,9 +357,9 @@
     wanted = [targets(c, r * RB + i) for i in range(RB)]
     twin_wanted = [targets(twin_c, r * RB + i) for i in range(RB)]
 
-    def square_step(g, accs):
-        out = []
-        for i in range(RB):
+    def square(i):
+        acc = jnp.zeros((64, 256), F32)
+        for g in range(4):
             t = [rows[g * 4 + s, i] for s in range(4)]
             s = [turn(v) for v in t]
             top = [jnp.where(left, t[0], s[1]), jnp.where(left, t[2], s[3])]
@@ -351,21 +368,23 @@
                 [jnp.concatenate(top, axis=1), jnp.concatenate(low, axis=1)], axis=0
             )
             inner = [(g * 4 + s) * SEG + bct_ref[g * 4 + s, r * RB + i] for s in range(4)]
-            out.append(accs[i] + product(lhs, inner, wanted[i]))
-        return tuple(out)
-
-    accs = lax.fori_loop(0, 4, square_step, (jnp.zeros((64, 256), F32),) * RB)
+            acc = acc + product(lhs, inner, wanted[i])
+        return acc
+
     mate_h = h + 1 - 2 * lax.rem(h, 2)
     mate = (r, x * 4 + mate_h)
 
     def slot(dx, e):
         return lax.rem(x + dx, 4) * 4 + (mate_h if e else h)
 
+    PARTS = ((0, 64), (64, 64), (128, 32), (160, 32))
+    PLUS = ((0, 3), (1, 2))
+
     def sq_at(dx, e, i):
-        return squares.at[slot(dx, e), pl.ds(64 * i, 64)]
+        return squares.at[slot(dx, e), pl.ds(*PARTS[i])]
 
     def sq_sem_at(dx, e, i):
-        return sq_sem.at[(dx * 2 + e) * 3 + i]
+        return sq_sem.at[(dx * 2 + e) * 4 + i]
 
     def sq_wait(dx, e, i):
         arrived(sq_at(dx, e, i), sq_sem_at(dx, e, i))
@@ -378,49 +397,53 @@
         for dx in (3, 1):
             step = 1 if dx == 3 else -1
             sq_wait(dx, e, i)
-            if (i in PLUS_PARTS[e]) == (step == 1):
+            if (i in PLUS[e]) == (step == 1):
                 push(sq_at(dx, e, i), sq_sem_at(2, e, i), dev(dx=step))
 
     def cubes(i, *tiles):
         row = r * RB + i
-        for dx, e in tiles:
-            p = slot(dx, e)
-            lhs = squares[p, pl.ds(64 * i, 64)]
-            inner = [p * SEG + pct_ref[p, u, row] for u in range(QS)]
-            v = product(lhs, inner, wanted[i])
-            w = product(lhs, inner, twin_wanted[i], twin_c, twin_hi, twin_lo)
-            first = (dx, e) == (0, 0)
-            cube[i] = v if first else cube[i] + v
-            twin_cube[i] = w if first else twin_cube[i] + w
+        for to, want, col, refs in (
+            (twin_cube, twin_wanted, twin_c, (twin_hi, twin_lo)), (cube, wanted, c, (dup_hi, dup_lo))
+        ):
+            for dx, e in tiles:
+                p = slot(dx, e)
+                inner = [p * SEG + pct_ref[p, u, row] for u in range(QS)]
+                v = product(squares[p, pl.ds(64 * i, 64)], inner, want[i], col, *refs)
+                to[i] = v if (dx, e) == (0, 0) else to[i] + v
+            if (2, 1) in tiles and to is twin_cube:
+                push(to.at[i], back_sem.at[i], twin, dst=back_cube.at[i])
 
     for i in range(RB):
-        squares[c, pl.ds(64 * i, 64)] = accs[i]
-        push(sq_at(0, 0, i), sq_sem_at(0, 1, i), mate)
-        sq_along_x(0, i)
-    ALL = (0,) + NEAR + FARTHER + (6,)
-    for dz in ALL:
-        other.unpack(dz, False, False)
-    for dz in ALL[:7]:
-        other.from_sibling(dz, False)
-    for i in range(RB):
-        sq_near_x(0, i)
-        sq_wait(0, 1, i)
-        sq_along_x(1, i)
-    for dz in ALL:
-        other.other_plane(dz)
-    for dz in ALL[7:]:
-        other.from_sibling(dz, False)
-    for i in range(RB):
-        sq_near_x(1, i)
-    for dz in ALL:
-        other.from_sibling(dz, True)
+        squares[c, pl.ds(64 * i, 64)] = square(i)
+        for part in (i,) if i < 2 else (2, 3):
+            push(sq_at(0, 0, part), sq_sem_at(0, 1, part), mate)
+            sq_along_x(0, part)
+    for dz in (3, -3):
+        other.both_from_z(dz)
+    for part in range(4):
+        sq_near_x(0, part)
+        sq_wait(0, 1, part)
+        sq_along_x(1, part)
+    for dz in (2, -2, 1, -1) + FARTHER:
+        other.both_from_z(dz)
+    for flip in (False, True):
+        other.opposite_from_z(flip)
+        other.to_sibling(half, flip)
+    for dz in (0,) + NEAR + FARTHER + (6,):
+        for flip in (False, True):
+            other.unpack(dz, flip, False)
+    for part in range(4):
+        sq_near_x(1, part)
+    for dz in (0,) + NEAR + FARTHER + (6,):
+        for flip in (False, True):
+            other.from_sibling(dz, flip)
     for i in range(RB):
         cubes(i, (0, 0), (3, 0), (1, 0), (0, 1))
     for i in range(RB):
-        sq_wait(2, 0, i)
-        sq_wait(2, 1, i)
+        for part in (i,) if i < 2 else (2, 3):
+            sq_wait(2, 0, part)
+            sq_wait(2, 1, part)
         cubes(i, (2, 0), (3, 1), (1, 1), (2, 1))
-        push(twin_cube.at[i], back_sem.at[i], twin, dst=back_cube.at[i])
     for i in range(RB):
         arrived(back_cube.at[i], back_sem.at[i])
 
@@ -462,15 +485,14 @@
             pltpu.VMEM((NB, 4, 16, 128), BF16),
             pltpu.VMEM((RB, 64, 256), F32),
             pltpu.VMEM((RB, 64, 256), F32),
-            pltpu.SemaphoreType.DMA((180,)),
-            pltpu.SemaphoreType.DMA((14,)),
+            pltpu.SemaphoreType.DMA((200,)),
+            pltpu.SemaphoreType.DMA((28,)),
             pltpu.SemaphoreType.DMA((13,)),
             pltpu.SemaphoreType.DMA((26,)),
             pltpu.SemaphoreType.DMA((48,)),
-            pltpu.SemaphoreType.DMA((24,)),
-            pltpu.SemaphoreType.DMA((1,)),
-            pltpu.SemaphoreType.DMA((14,)),
-            pltpu.SemaphoreType.DMA((13,)),
+            pltpu.SemaphoreType.DMA((32,)),
+            pltpu.SemaphoreType.DMA((2,)),
+            pltpu.SemaphoreType.DMA((28,)),
             pltpu.SemaphoreType.DMA((26,)),
             pltpu.SemaphoreType.DMA((3,)),
         ],

time: 73.9 us -> 71.6 us (0.969)
  the two profiles are of different devices: /device:TPU:17 before, /device:TPU:8 now
where the time goes in v4:
time: 71.6 us; the launch traced here: 71.2 us
  Pallas kernels  69.5 us (97%)
  local copies, waits for them, and re-layouts  1.62 us (2%)
    pallas_call x1, Pallas kernels, per_device(): pl.pallas_call(kernel, out_shape=jax.ShapeDtypeStruct((RB, 32, QS, 128),...  69.5 us
    unnamed x1, local copies, waits for them, and re-layouts  1.62 us

profile of v4, /device:TPU:8, one launch (start us, length us, event | category | flops | bytes accessed | tf_op | source)
XLA Modules:
  0.0 71.2 jit_solution(991431666590650124)
XLA Ops:
  0.0 69.5 %shard_map.46 = f32[3,32,4,128]{3,2,1,0:T(4,128)} custom-call(f32[3,32,128]{2,1,0:T(8,128)} %bitcast.8, s32[16,144]{1,0:T(8,128)} %bitcast.9, s32[16,4,144]{2,1,0:T(4,128)} %bitcast.7, s32[144]{0:T(256)} %size_hbm.1), custom_call_target="tpu_custom_call" | custom-call | tf_op jit(solution)/shard_map/pallas_call | solution.py:465
  69.5 1.6 %copy.6 = f32[3,1,4,4096]{3,2,1,0:T(4,128)} copy(f32[3,1,4,4096]{3,2,1,0:T(4,128)} %bitcast.6) | data formatting | bytes 393216
